TPU v7x, 32 devices: a whole 2x2x4 slice. The times are simulated.
32 devices in a mesh: cache: 4 (over y, core), dev: 8 (over z, x).
Axes of the slice: x: 2, y: 2, z: 4, core: 2. Of those that a mesh axis runs over, the one named last changes fastest.
Arguments:
- queries: bfloat16 [4, 1024, 8192], P('cache', None, 'dev'), may hold values from -8 to 8
- store_kv: bfloat16 [128, 512, 2048], P('cache', 'dev'), may hold values from -4 to 4
- self_kv: bfloat16 [4, 1024, 2048], P('cache'), may hold values from -5 to 5
- rec_states: bfloat16 [4, 512, 8192], P('cache', None, 'dev'), may hold values from -400 to 400
- norm_gain: bfloat16 [8192], P('dev'), may hold values from 0.099609375 to 1.8984375
- w_kv: bfloat16 [8192, 2048], P('dev'), may hold values from -0.0625 to 0.0625
- retrieval: int32 [4, 16], replicated, may hold values from 0 to 127, as said below
- doc_home: int32 [128], replicated, may hold values from 0 to 127, as said below
- rec_index: int32 [4, 16, 32], P('cache'), may hold values from 0 to 511, as said below
Outputs:
- attended: bfloat16 [4, 1024, 8192], P('cache', None, 'dev')
Inputs may be any that keep to these rules, and one draw needn't show every extreme that they name: `retrieval`: each request names 16 distinct documents; their store rows lie in exactly 4 of the groups of 32 consecutive rows, 4 in each. `doc_home`: every store row holds exactly one document. `rec_index`: the 32 positions of one block are distinct.
All inputs are finite; a program needn't handle non-finite values.
Results may differ from a plain program's by a relative error of at most 0.0045.
Values may be sent and summed in bfloat16 or wider, within the bound.
A program may use at most 128 MiB of HBM per device.

v0:
```python
import math

import jax
import jax.numpy as jnp
from jax import lax
from jax.sharding import PartitionSpec as P

D = 8192
QH = 64
KVH = 8
HD = 128
RET = 16
CAP = 4
REC = 32
DOC_GRP = 32


eps_norm = 1e-05
tile_rows = 512


def own_head(wide_rows, head_count, head_size, chosen):
    shaped = wide_rows.reshape(wide_rows.shape[:-1] + (2, head_count, head_size))
    taken = lax.dynamic_index_in_dim(shaped, chosen, shaped.ndim - 2, keepdims=False)
    return taken.reshape(wide_rows.shape[:-1] + (2 * head_size,))


def pick_heads(wide_rows, head_count, head_size, chosen):
    shaped = wide_rows.reshape(wide_rows.shape[:-1] + (2, head_count, head_size))
    taken = jnp.take(shaped, chosen, axis=shaped.ndim - 2)
    moved = jnp.moveaxis(taken, shaped.ndim - 2, 0)
    return moved.reshape(moved.shape[:-2] + (2 * head_size,))


def shards(queries, store_kv, self_kv, rec_states, norm_gain, w_kv, retrieval, doc_home, rec_index):
    groups = lax.axis_size("cache")
    members = lax.axis_size("dev")
    my_group = lax.axis_index("cache")
    my_member = lax.axis_index("dev")
    per_device = QH // members
    ratio_heads = QH // KVH
    my_head = my_member * per_device // ratio_heads
    shard_rows = store_kv.shape[1]
    kv_width = store_kv.shape[2]
    inv_root = 1.0 / math.sqrt(HD)
    stored_at = jnp.take(doc_home, retrieval, axis=0)
    source = stored_at // DOC_GRP
    local_row = stored_at % DOC_GRP
    before = jnp.arange(RET)[None, :] < jnp.arange(RET)[:, None]
    same_home = source[:, :, None] == source[:, None, :]
    rank_within = jnp.sum((same_home & before[None, :, :]).astype(jnp.int32), axis=2)
    places = jnp.arange(CAP, dtype=jnp.int32)
    matching = (source[:, None, :] == my_group) & (rank_within[:, None, :] == places[None, :, None])
    pick_row = jnp.sum(jnp.where(matching, local_row[:, None, :], 0), axis=2)
    filled = jnp.any(matching, axis=2)
    outgoing = jnp.take(store_kv, pick_row.reshape(-1), axis=0).reshape(
        groups, CAP, shard_rows, kv_width
    )
    outgoing = jnp.where(filled[:, :, None, None], outgoing, jnp.zeros((), store_kv.dtype))
    my_source = lax.dynamic_index_in_dim(source, my_group, 0, keepdims=False)
    my_rank = lax.dynamic_index_in_dim(rank_within, my_group, 0, keepdims=False)
    slot_place = my_source * CAP + my_rank
    dest_heads = jnp.arange(members, dtype=jnp.int32) * per_device // ratio_heads
    arrived = lax.all_to_all(outgoing, "cache", split_axis=0, concat_axis=0, tiled=True)
    compact = jnp.take(arrived.reshape(groups * CAP, shard_rows, kv_width), slot_place, axis=0)
    spread = pick_heads(compact, KVH, HD, dest_heads)
    fetched = lax.all_to_all(spread, "dev", split_axis=0, concat_axis=2, tiled=True)[0]
    states = rec_states[0].astype(jnp.float32)
    partial_sq = jnp.sum(states * states, axis=1)
    total_sq = lax.psum(partial_sq, "dev")
    inv_rms = lax.rsqrt(total_sq / D + eps_norm)
    normed = (states * norm_gain.astype(jnp.float32)[None, :] * inv_rms[:, None]).astype(
        jnp.bfloat16
    )
    summed = lax.psum(jnp.dot(normed, w_kv, preferred_element_type=jnp.float32), "dev")
    redone = summed.astype(jnp.bfloat16)
    own_rows = own_head(redone.reshape(RET, REC, kv_width), KVH, HD, my_head)
    full_block = fetched.shape[1]
    positions = rec_index[0]
    onehot = positions[:, :, None] == jnp.arange(full_block, dtype=jnp.int32)[None, None, :]
    placed = jnp.einsum(
        "kib,kic->kbc", onehot.astype(jnp.bfloat16), own_rows, preferred_element_type=jnp.float32
    ).astype(jnp.bfloat16)
    replaced_at = jnp.any(onehot, axis=1)
    blocks = jnp.where(replaced_at[:, :, None], placed, fetched)
    doc_keys = blocks[:, :, :HD].reshape(-1, HD)
    doc_values = blocks[:, :, HD:].reshape(-1, HD)
    own_self = own_head(self_kv[0], KVH, HD, my_head)
    self_keys = own_self[:, :HD]
    self_values = own_self[:, HD:]
    prompt = queries.shape[1]
    head_rows = jnp.transpose(queries[0].reshape(prompt, per_device, HD), (1, 0, 2))
    block_len = min(tile_rows, prompt)
    block_count = prompt // block_len
    key_spots = jnp.arange(prompt, dtype=jnp.int32)

    def attend(pair_index):
        head_at = pair_index // block_count
        first_row = pair_index % block_count * block_len
        query_block = lax.dynamic_slice_in_dim(
            lax.dynamic_index_in_dim(head_rows, head_at, 0, keepdims=False), first_row, block_len, 0
        )
        doc_scores = (
            jnp.einsum("qd,kd->qk", query_block, doc_keys, preferred_element_type=jnp.float32)
            * inv_root
        )
        self_scores = (
            jnp.einsum("qd,kd->qk", query_block, self_keys, preferred_element_type=jnp.float32)
            * inv_root
        )
        allowed = (
            key_spots[None, :] <= (first_row + jnp.arange(block_len, dtype=jnp.int32))[:, None]
        )
        self_scores = jnp.where(allowed, self_scores, -jnp.inf)
        top = jnp.maximum(jnp.max(doc_scores, axis=1), jnp.max(self_scores, axis=1))
        doc_expd = jnp.exp(doc_scores - top[:, None])
        self_expd = jnp.exp(self_scores - top[:, None])
        total = jnp.sum(doc_expd, axis=1) + jnp.sum(self_expd, axis=1)
        weighted = jnp.dot(
            doc_expd.astype(jnp.bfloat16), doc_values, preferred_element_type=jnp.float32
        )
        weighted = weighted + jnp.dot(
            self_expd.astype(jnp.bfloat16), self_values, preferred_element_type=jnp.float32
        )
        return (weighted / total[:, None]).astype(jnp.bfloat16)

    gathered_out = lax.map(attend, jnp.arange(per_device * block_count, dtype=jnp.int32))
    result = jnp.transpose(gathered_out.reshape(per_device, prompt, HD), (1, 0, 2))
    return result.reshape(1, prompt, per_device * HD)


def solution(mesh):
    placed = (
        P("cache", None, "dev"),
        P("cache", "dev", None),
        P("cache", None, None),
        P("cache", None, "dev"),
        P("dev"),
        P("dev", None),
        P(),
        P(),
        P("cache", None, None),
    )
    return jax.shard_map(
        shards, mesh=mesh, in_specs=placed, out_specs=P("cache", None, "dev"), check_vma=False
    )
```

profile of v0, /device:TPU:17, one launch (start us, length us, event | category | flops | bytes accessed | tf_op | source)
XLA Modules:
  0.0 938.7 jit_solution(14967193840605739023)
XLA Ops:
  20.1 47.3 %all-to-all-done = bf16[4,4,64,2048]{3,2,1,0:T(8,128)(2,1)} async-done(((bf16[4,4,64,2048]{3,2,1,0:T(8,128)(2,1)}), bf16[4,4,64,2048]{3,2,1,0:T(8,128)(2,1)}, u32[]{:S(2)}, u32[]{:S(2)}) %all-to-all-start) | async-done | bytes 4194336 | tf_op jit(solution)/shard_map/all_to_all | solution.py:64
  95.7 97.1 %psum.14 = f32[512]{0:T(512)S(1)} all-reduce(f32[512]{0:T(512)S(1)} %fusion.24), channel_id=1, replica_groups=mesh['cache'=4,'dev'=8] {'dev'}, use_global_device_ids=true, to_apply=%region_2.3 | all-reduce | flops 512 | bytes 4096 | tf_op jit(solution)/shard_map/psum | solution.py:70
  199.4 163.0 %all-reduce.1 = bf16[512,2048]{1,0:T(8,128)(2,1)S(1)} all-reduce(f32[512,2048]{1,0:T(8,128)} %fusion.25), channel_id=1, replica_groups=mesh['cache'=4,'dev'=8] {'dev'}, use_global_device_ids=true, to_apply=%region_3.4 | all-reduce | flops 1048576 | bytes 6291456 | tf_op jit(solution)/shard_map/psum | solution.py:75
  386.7 546.8 %while.14 = (s32[]{:T(128)}, bf16[16,512,128]{2,1,0:T(8,128)(2,1)}, s32[16]{0:T(128)S(1)}, bf16[8,1024,128]{1,2,0:T(8,128)(2,1)}, bf16[8192,128]{1,0:T(8,128)(2,...) while((s32[]{:T(128)}, bf16[16,512,128]{2,1,0:T(8,128)(2,1)}, ...), condition=%wide.region_12.13_spmd.clone, body=%wide.region_7.12_spmd.clone.sunk | while | flops 2453863936 | bytes 79072280 | solution.py:127
  389.8 9.9 %multiply_reduce_fusion.2 = (f32[512]{0:T(512)S(1)}, f32[512,8192]{1,0:T(8,128)}) fusion(bf16[8192,128]{1,0:T(8,128)(2,1)} %get-tuple-element.318, bf16[8,1024,128]{1,2,0:T(8,128)(2,1)} %get-tuple-element.317, s32[]{:T(128)S(6)} %select_n.272, s32[]{:T(128)S(6)} %select_n.275), kind=kOutput, calls=%fused_computation.6.clone.1 | convolution fusion | flops 1082129920 | bytes 19007496 | tf_op jit(solution)/shard_map/while/body/eval_jaxpr/qd,kd->qk/dot_general | solution.py:104
  403.3 8.6 fusion.69
  424.0 9.9 %multiply_reduce_fusion.2 = (f32[512]{0:T(512)S(1)}, f32[512,8192]{1,0:T(8,128)}) fusion(bf16[8192,128]{1,0:T(8,128)(2,1)} %get-tuple-element.318, bf16[8,1024,128]{1,2,0:T(8,128)(2,1)} %get-tuple-element.317, s32[]{:T(128)S(6)} %select_n.272, s32[]{:T(128)S(6)} %select_n.275), kind=kOutput, calls=%fused_computation.6.clone.1 | convolution fusion | flops 1082129920 | bytes 19007496 | tf_op jit(solution)/shard_map/while/body/eval_jaxpr/qd,kd->qk/dot_general | solution.py:104
  437.4 8.6 fusion.69
  458.1 9.9 %multiply_reduce_fusion.2 = (f32[512]{0:T(512)S(1)}, f32[512,8192]{1,0:T(8,128)}) fusion(bf16[8192,128]{1,0:T(8,128)(2,1)} %get-tuple-element.318, bf16[8,1024,128]{1,2,0:T(8,128)(2,1)} %get-tuple-element.317, s32[]{:T(128)S(6)} %select_n.272, s32[]{:T(128)S(6)} %select_n.275), kind=kOutput, calls=%fused_computation.6.clone.1 | convolution fusion | flops 1082129920 | bytes 19007496 | tf_op jit(solution)/shard_map/while/body/eval_jaxpr/qd,kd->qk/dot_general | solution.py:104
  471.6 8.6 fusion.69
  492.3 9.9 %multiply_reduce_fusion.2 = (f32[512]{0:T(512)S(1)}, f32[512,8192]{1,0:T(8,128)}) fusion(bf16[8192,128]{1,0:T(8,128)(2,1)} %get-tuple-element.318, bf16[8,1024,128]{1,2,0:T(8,128)(2,1)} %get-tuple-element.317, s32[]{:T(128)S(6)} %select_n.272, s32[]{:T(128)S(6)} %select_n.275), kind=kOutput, calls=%fused_computation.6.clone.1 | convolution fusion | flops 1082129920 | bytes 19007496 | tf_op jit(solution)/shard_map/while/body/eval_jaxpr/qd,kd->qk/dot_general | solution.py:104
  505.8 8.6 fusion.69
  526.5 9.9 %multiply_reduce_fusion.2 = (f32[512]{0:T(512)S(1)}, f32[512,8192]{1,0:T(8,128)}) fusion(bf16[8192,128]{1,0:T(8,128)(2,1)} %get-tuple-element.318, bf16[8,1024,128]{1,2,0:T(8,128)(2,1)} %get-tuple-element.317, s32[]{:T(128)S(6)} %select_n.272, s32[]{:T(128)S(6)} %select_n.275), kind=kOutput, calls=%fused_computation.6.clone.1 | convolution fusion | flops 1082129920 | bytes 19007496 | tf_op jit(solution)/shard_map/while/body/eval_jaxpr/qd,kd->qk/dot_general | solution.py:104
  539.9 8.6 fusion.69
  560.7 9.9 %multiply_reduce_fusion.2 = (f32[512]{0:T(512)S(1)}, f32[512,8192]{1,0:T(8,128)}) fusion(bf16[8192,128]{1,0:T(8,128)(2,1)} %get-tuple-element.318, bf16[8,1024,128]{1,2,0:T(8,128)(2,1)} %get-tuple-element.317, s32[]{:T(128)S(6)} %select_n.272, s32[]{:T(128)S(6)} %select_n.275), kind=kOutput, calls=%fused_computation.6.clone.1 | convolution fusion | flops 1082129920 | bytes 19007496 | tf_op jit(solution)/shard_map/while/body/eval_jaxpr/qd,kd->qk/dot_general | solution.py:104
  574.1 8.6 fusion.69
  594.8 9.9 %multiply_reduce_fusion.2 = (f32[512]{0:T(512)S(1)}, f32[512,8192]{1,0:T(8,128)}) fusion(bf16[8192,128]{1,0:T(8,128)(2,1)} %get-tuple-element.318, bf16[8,1024,128]{1,2,0:T(8,128)(2,1)} %get-tuple-element.317, s32[]{:T(128)S(6)} %select_n.272, s32[]{:T(128)S(6)} %select_n.275), kind=kOutput, calls=%fused_computation.6.clone.1 | convolution fusion | flops 1082129920 | bytes 19007496 | tf_op jit(solution)/shard_map/while/body/eval_jaxpr/qd,kd->qk/dot_general | solution.py:104
  608.3 8.6 fusion.69
  629.0 9.9 %multiply_reduce_fusion.2 = (f32[512]{0:T(512)S(1)}, f32[512,8192]{1,0:T(8,128)}) fusion(bf16[8192,128]{1,0:T(8,128)(2,1)} %get-tuple-element.318, bf16[8,1024,128]{1,2,0:T(8,128)(2,1)} %get-tuple-element.317, s32[]{:T(128)S(6)} %select_n.272, s32[]{:T(128)S(6)} %select_n.275), kind=kOutput, calls=%fused_computation.6.clone.1 | convolution fusion | flops 1082129920 | bytes 19007496 | tf_op jit(solution)/shard_map/while/body/eval_jaxpr/qd,kd->qk/dot_general | solution.py:104
  642.5 8.6 fusion.69
  663.2 9.9 %multiply_reduce_fusion.2 = (f32[512]{0:T(512)S(1)}, f32[512,8192]{1,0:T(8,128)}) fusion(bf16[8192,128]{1,0:T(8,128)(2,1)} %get-tuple-element.318, bf16[8,1024,128]{1,2,0:T(8,128)(2,1)} %get-tuple-element.317, s32[]{:T(128)S(6)} %select_n.272, s32[]{:T(128)S(6)} %select_n.275), kind=kOutput, calls=%fused_computation.6.clone.1 | convolution fusion | flops 1082129920 | bytes 19007496 | tf_op jit(solution)/shard_map/while/body/eval_jaxpr/qd,kd->qk/dot_general | solution.py:104
  676.6 8.6 fusion.69
  697.3 9.9 %multiply_reduce_fusion.2 = (f32[512]{0:T(512)S(1)}, f32[512,8192]{1,0:T(8,128)}) fusion(bf16[8192,128]{1,0:T(8,128)(2,1)} %get-tuple-element.318, bf16[8,1024,128]{1,2,0:T(8,128)(2,1)} %get-tuple-element.317, s32[]{:T(128)S(6)} %select_n.272, s32[]{:T(128)S(6)} %select_n.275), kind=kOutput, calls=%fused_computation.6.clone.1 | convolution fusion | flops 1082129920 | bytes 19007496 | tf_op jit(solution)/shard_map/while/body/eval_jaxpr/qd,kd->qk/dot_general | solution.py:104
  710.8 8.6 fusion.69
  731.5 9.9 %multiply_reduce_fusion.2 = (f32[512]{0:T(512)S(1)}, f32[512,8192]{1,0:T(8,128)}) fusion(bf16[8192,128]{1,0:T(8,128)(2,1)} %get-tuple-element.318, bf16[8,1024,128]{1,2,0:T(8,128)(2,1)} %get-tuple-element.317, s32[]{:T(128)S(6)} %select_n.272, s32[]{:T(128)S(6)} %select_n.275), kind=kOutput, calls=%fused_computation.6.clone.1 | convolution fusion | flops 1082129920 | bytes 19007496 | tf_op jit(solution)/shard_map/while/body/eval_jaxpr/qd,kd->qk/dot_general | solution.py:104
  765.7 9.9 %multiply_reduce_fusion.2 = (f32[512]{0:T(512)S(1)}, f32[512,8192]{1,0:T(8,128)}) fusion(bf16[8192,128]{1,0:T(8,128)(2,1)} %get-tuple-element.318, bf16[8,1024,128]{1,2,0:T(8,128)(2,1)} %get-tuple-element.317, s32[]{:T(128)S(6)} %select_n.272, s32[]{:T(128)S(6)} %select_n.275), kind=kOutput, calls=%fused_computation.6.clone.1 | convolution fusion | flops 1082129920 | bytes 19007496 | tf_op jit(solution)/shard_map/while/body/eval_jaxpr/qd,kd->qk/dot_general | solution.py:104
  799.9 9.9 %multiply_reduce_fusion.2 = (f32[512]{0:T(512)S(1)}, f32[512,8192]{1,0:T(8,128)}) fusion(bf16[8192,128]{1,0:T(8,128)(2,1)} %get-tuple-element.318, bf16[8,1024,128]{1,2,0:T(8,128)(2,1)} %get-tuple-element.317, s32[]{:T(128)S(6)} %select_n.272, s32[]{:T(128)S(6)} %select_n.275), kind=kOutput, calls=%fused_computation.6.clone.1 | convolution fusion | flops 1082129920 | bytes 19007496 | tf_op jit(solution)/shard_map/while/body/eval_jaxpr/qd,kd->qk/dot_general | solution.py:104
  813.3 8.6 fusion.69
  834.0 9.9 %multiply_reduce_fusion.2 = (f32[512]{0:T(512)S(1)}, f32[512,8192]{1,0:T(8,128)}) fusion(bf16[8192,128]{1,0:T(8,128)(2,1)} %get-tuple-element.318, bf16[8,1024,128]{1,2,0:T(8,128)(2,1)} %get-tuple-element.317, s32[]{:T(128)S(6)} %select_n.272, s32[]{:T(128)S(6)} %select_n.275), kind=kOutput, calls=%fused_computation.6.clone.1 | convolution fusion | flops 1082129920 | bytes 19007496 | tf_op jit(solution)/shard_map/while/body/eval_jaxpr/qd,kd->qk/dot_general | solution.py:104
  868.2 9.9 %multiply_reduce_fusion.2 = (f32[512]{0:T(512)S(1)}, f32[512,8192]{1,0:T(8,128)}) fusion(bf16[8192,128]{1,0:T(8,128)(2,1)} %get-tuple-element.318, bf16[8,1024,128]{1,2,0:T(8,128)(2,1)} %get-tuple-element.317, s32[]{:T(128)S(6)} %select_n.272, s32[]{:T(128)S(6)} %select_n.275), kind=kOutput, calls=%fused_computation.6.clone.1 | convolution fusion | flops 1082129920 | bytes 19007496 | tf_op jit(solution)/shard_map/while/body/eval_jaxpr/qd,kd->qk/dot_general | solution.py:104
  881.7 8.6 fusion.69
  902.4 9.9 %multiply_reduce_fusion.2 = (f32[512]{0:T(512)S(1)}, f32[512,8192]{1,0:T(8,128)}) fusion(bf16[8192,128]{1,0:T(8,128)(2,1)} %get-tuple-element.318, bf16[8,1024,128]{1,2,0:T(8,128)(2,1)} %get-tuple-element.317, s32[]{:T(128)S(6)} %select_n.272, s32[]{:T(128)S(6)} %select_n.275), kind=kOutput, calls=%fused_computation.6.clone.1 | convolution fusion | flops 1082129920 | bytes 19007496 | tf_op jit(solution)/shard_map/while/body/eval_jaxpr/qd,kd->qk/dot_general | solution.py:104
  (259 shorter events, 328.6 us)
Async XLA Ops:
  14.5 52.9 %all-to-all-start = ((bf16[4,4,64,2048]{3,2,1,0:T(8,128)(2,1)}), bf16[4,4,64,2048]{3,2,1,0:T(8,128)(2,1)}, u32[]{:S(2)}, u32[]{:S(2)}) async-start(bf16[4,4,64,2048]{3,2,1,0:T(8,128)(2,1)} %select_select_fusion), calls=%async_computation | async-start | bytes 8388608 | tf_op jit(solution)/shard_map/all_to_all | solution.py:64
  89.7 5.7 copy-start.7
  89.7 5.7 copy-start.5
  89.7 289.0 %all-to-all-start.1 = ((bf16[8,16,64,256]{3,2,1,0:T(8,128)(2,1)}), bf16[8,16,64,256]{3,2,1,0:T(8,128)(2,1)}, u32[]{:S(2)}, u32[]{:S(2)}) async-start(bf16[8,16,64,256]{3,2,1,0:T(8,128)(2,1)} %copy_bitcast_fusion), calls=%async_computation.1 | async-start | bytes 8388608 | tf_op jit(solution)/shard_map/all_to_all | solution.py:67
  368.1 7.6 copy-start.4
  371.8 6.4 copy-start.6
  401.5 1.3 copy-start.2
  411.9 7.8 copy-start.3
  435.6 1.3 copy-start.2
  446.0 7.8 copy-start.3
  469.8 1.3 copy-start.2
  480.2 7.8 copy-start.3
  514.4 7.8 copy-start.3
  538.1 1.3 copy-start.2
  548.6 7.8 copy-start.3
  582.7 7.8 copy-start.3
  606.5 1.3 copy-start.2
  616.9 7.8 copy-start.3
  651.1 7.8 copy-start.3
  685.3 7.8 copy-start.3
  709.0 1.3 copy-start.2
  719.4 7.8 copy-start.3
  753.6 7.8 copy-start.3
  777.3 1.3 copy-start.2
  787.8 7.8 copy-start.3
  822.0 7.8 copy-start.3
  845.7 1.3 copy-start.2
  856.1 7.8 copy-start.3
  879.9 1.3 copy-start.2
  890.3 7.8 copy-start.3
  924.5 7.8 copy-start.3
  933.5 5.3 copy-start.1
  (8 other events, 10.1 us)
where the time goes:
time: 947 us; the launch traced here: 939 us
  matrix products  339 us (36%)
  blocking collectives  260 us (27%)
  other arithmetic  162 us (17%)
  local copies, waits for them, and re-layouts  78.1 us (8%)
  waiting for transfers between devices  47.3 us (5%)
  loops' own time  40.3 us (4%)
  starting transfers between devices  11.2 us (1%)
    psum x1, blocking collectives, shards(): lax.psum(jnp.dot(normed, w_kv, preferred_element_type=jnp.float32), 'dev')  163 us
    dot_general x16, matrix products, attend(): jnp.einsum('qd,kd->qk', query_block, doc_keys, preferred_element_type=jnp...  159 us
    reduce_sum x32, other arithmetic, attend(): total = jnp.sum(doc_expd, axis=1) + jnp.sum(self_expd, axis=1)  146 us
    dot_general x16, matrix products, attend(): jnp.dot(doc_expd.astype(jnp.bfloat16), doc_values, preferred_element_type...  125 us
    psum x1, blocking collectives, shards(): total_sq = lax.psum(partial_sq, 'dev')  97.1 us
    all_to_all x1, waiting for transfers between devices, shards(): lax.all_to_all(outgoing, 'cache', split_axis=0, concat_axis=0, tiled=True)  47.3 us
    another operation x1, loops' own time, shards(): lax.map(attend, jnp.arange(per_device * block_count, dtype=jnp.int32))  40.3 us
    dot_general x16, matrix products, attend(): jnp.einsum('qd,kd->qk', query_block, self_keys, preferred_element_type=jn...  27.7 us
  transfers between devices with their start and end apart: 2, of which 1 were waited for; matrix products, arithmetic and copies ran while one was open for 2% of the time, Pallas kernels for 0%

commit v1 on v0

v1 whole, which is shorter than its diff:
```python
import functools
import math

import jax
import jax.numpy as jnp
from jax import lax
from jax.experimental import pallas as pl
from jax.experimental.pallas import tpu as pltpu
from jax.sharding import PartitionSpec as P

D = 8192
QH = 64
KVH = 8
HD = 128
RET = 16
CAP = 4
REC = 32
DOC_GRP = 32

eps_norm = 1e-05
MESH = pl.DeviceIdType.MESH
TQ = 256
REMOTE = True


def flip(index, bits, count):
    out = 0
    step = 1
    while step < count:
        digit = index // step % 2
        if bits // step % 2:
            digit = 1 - digit
        out = out + digit * step
        step *= 2
    return out


def gather_kernel(rows_ref, store_ref, out_ref):
    for head in range(KVH):
        out_ref[head, 0, :, :HD] = store_ref[0, :, head * HD : (head + 1) * HD]
        out_ref[head, 0, :, HD:] = store_ref[0, :, (KVH + head) * HD : (KVH + head + 1) * HD]


def gather_blocks(pick_row, store_kv, groups):
    tok, width = store_kv.shape[1:]
    return pl.pallas_call(
        gather_kernel,
        grid_spec=pltpu.PrefetchScalarGridSpec(
            num_scalar_prefetch=1,
            grid=(groups * CAP,),
            in_specs=[pl.BlockSpec((1, tok, width), lambda i, rows: (rows[i], 0, 0))],
            out_specs=pl.BlockSpec(
                (KVH, 1, tok, 2 * HD), lambda i, rows: (0, i // CAP, i % CAP, 0)
            ),
        ),
        out_shape=jax.ShapeDtypeStruct((KVH, groups, CAP * tok, 2 * HD), store_kv.dtype),
    )(pick_row, store_kv)


def nt(a, b):
    return lax.dot_general(a, b, (((1,), (1,)), ((), ())), preferred_element_type=jnp.float32)


def split_queries(q_ref, q2_ref, heads, prompt):
    scale = math.log2(math.e) / math.sqrt(HD)
    for head in range(heads):
        scaled = q_ref[:, head * HD : (head + 1) * HD].astype(jnp.float32) * scale
        high = scaled.astype(jnp.bfloat16)
        low = (scaled - high.astype(jnp.float32)).astype(jnp.bfloat16)
        q2_ref[head * prompt : (head + 1) * prompt, :HD] = high
        q2_ref[head * prompt : (head + 1) * prompt, HD:] = low


def self_pass(q2_ref, self_ref, k2_ref, v2_ref, acc_ref, top_ref, heads, prompt):
    keys = self_ref[:, :HD]
    k2_ref[:prompt, :HD] = keys
    k2_ref[:prompt, HD:] = keys
    v2_ref[:prompt, :HD] = self_ref[:, HD:]
    v2_ref[:prompt, HD:] = jnp.ones((prompt, HD), jnp.bfloat16)

    @pl.loop(0, heads)
    def _(head):
        for tile in range(prompt // TQ):
            width = (tile + 1) * TQ
            rows = pl.ds(pl.multiple_of(head * prompt + tile * TQ, TQ), TQ)
            scores = nt(q2_ref[rows, :], k2_ref[:width, :])
            at = lax.broadcasted_iota(jnp.int32, (TQ, width), 0) + tile * TQ
            key = lax.broadcasted_iota(jnp.int32, (TQ, width), 1)
            scores = jnp.where(key <= at, scores, -jnp.inf)
            top = jnp.max(scores, axis=1, keepdims=True)
            expd = jnp.exp2(scores - top).astype(jnp.bfloat16)
            acc_ref[rows, :] = jnp.dot(
                expd, v2_ref[:width, :], preferred_element_type=jnp.float32
            )
            top_ref[rows, :] = jnp.broadcast_to(top, (TQ, HD))


def block_pass(q2_ref, k2_ref, v2_ref, acc_ref, top_ref, rows_total, count, unroll=2):
    @pl.loop(0, rows_total // (TQ * unroll))
    def _(step):
        spans = [
            pl.ds(pl.multiple_of(step * (TQ * unroll) + part * TQ, TQ), TQ)
            for part in range(unroll)
        ]
        scores = [nt(q2_ref[rows, :], k2_ref[:count, :]) for rows in spans]
        for rows, score in zip(spans, scores):
            before = top_ref[rows, :]
            top = jnp.maximum(before, jnp.max(score, axis=1, keepdims=True))
            expd = jnp.exp2(score - top[:, :1]).astype(jnp.bfloat16)
            fade = jnp.exp2(before - top)
            fresh = jnp.dot(expd, v2_ref[:count, :], preferred_element_type=jnp.float32)
            acc_ref[rows, :HD] = acc_ref[rows, :HD] * fade + fresh[:, :HD]
            acc_ref[rows, HD:] = acc_ref[rows, HD:] * fade + fresh[:, HD:]
            top_ref[rows, :] = top


def neutral(kv, keep, first_key, k2_ref, v2_ref, base):
    count = kv.shape[0]
    keys = kv[:, :HD] * keep + first_key * (1 - keep)
    k2_ref[base : base + count, :HD] = keys
    k2_ref[base : base + count, HD:] = keys
    v2_ref[base : base + count, :HD] = kv[:, HD:] * keep
    v2_ref[base : base + count, HD:] = keep


def finish(acc_ref, out_ref, heads, prompt):
    @pl.loop(0, prompt // TQ)
    def _(tile):
        rows = pl.ds(pl.multiple_of(tile * TQ, TQ), TQ)
        for head in range(heads):
            part = pl.ds(pl.multiple_of(head * prompt + tile * TQ, TQ), TQ)
            out_ref[rows, head * HD : (head + 1) * HD] = (
                acc_ref[part, :HD] / acc_ref[part, HD:]
            ).astype(out_ref.dtype)


def plain_kernel(heads, prompt, chunk, q_ref, self_ref, kv_ref, keep_ref, rec_ref, out_ref,
                 q2_ref, k2_ref, v2_ref, acc_ref, top_ref):
    split_queries(q_ref, q2_ref, heads, prompt)
    self_pass(q2_ref, self_ref, k2_ref, v2_ref, acc_ref, top_ref, heads, prompt)
    first_key = self_ref[0:1, :HD]

    @pl.loop(0, kv_ref.shape[0] // chunk)
    def _(at):
        rows = pl.ds(pl.multiple_of(at * chunk, chunk), chunk)
        neutral(kv_ref[rows, :], keep_ref[rows, :], first_key, k2_ref, v2_ref, 0)
        block_pass(q2_ref, k2_ref, v2_ref, acc_ref, top_ref, heads * prompt, chunk)

    count = rec_ref.shape[0]
    neutral(rec_ref[...], jnp.ones((count, HD), jnp.bfloat16), first_key, k2_ref, v2_ref, 0)
    block_pass(q2_ref, k2_ref, v2_ref, acc_ref, top_ref, heads * prompt, count)
    finish(acc_ref, out_ref, heads, prompt)


def state_scratch(rows, chunk):
    return [
        pltpu.VMEM((rows, 2 * HD), jnp.bfloat16),
        pltpu.VMEM((chunk, 2 * HD), jnp.bfloat16),
        pltpu.VMEM((chunk, 2 * HD), jnp.bfloat16),
        pltpu.VMEM((rows, 2 * HD), jnp.float32),
        pltpu.VMEM((rows, HD), jnp.float32),
    ]


def plain_attention(q, own_self, kv, keep, rec):
    prompt, width = q.shape
    heads = width // HD
    chunk = min(2048, kv.shape[0])
    vmem = pl.BlockSpec(memory_space=pltpu.VMEM)
    return pl.pallas_call(
        functools.partial(plain_kernel, heads, prompt, chunk),
        out_shape=jax.ShapeDtypeStruct((prompt, width), jnp.bfloat16),
        in_specs=[vmem] * 5,
        out_specs=vmem,
        scratch_shapes=state_scratch(heads * prompt, chunk),
        compiler_params=pltpu.CompilerParams(vmem_limit_bytes=60 * 1024 * 1024),
    )(q, own_self, kv, keep, rec)


def remote_kernel(heads, prompt, groups, members, q_ref, self_ref, keep_ref, x_ref, sq_ref, w_ref,
                  sent_ref, out_ref, q2_ref, k2_ref, v2_ref, acc_ref, top_ref, kv_ref, part_ref,
                  near_ref, mid_ref, far_ref, sums_ref, kv_send, kv_recv, near_send, near_recv,
                  far_send, far_recv, sq_send, sq_recv, local_sem):
    my_group = lax.axis_index("cache")
    me = lax.axis_index("dev")
    rec_rows = x_ref.shape[0]
    half = members // 2
    own = pltpu.make_async_copy(sent_ref.at[me, my_group], kv_ref.at[0, 0], local_sem)
    own.start()

    barrier = pltpu.get_barrier_semaphore()
    for k in range(members):
        for j in range(groups):
            if k or j:
                pl.semaphore_signal(
                    barrier, inc=1,
                    device_id={"cache": flip(my_group, j, groups), "dev": flip(me, k, members)},
                    device_id_type=MESH,
                )

    @pl.loop(0, members)
    def _(head):
        for side in range(2):
            cols = pl.ds(pl.multiple_of((side * KVH + head) * HD, HD), HD)
            part_ref[head, :, side * HD : (side + 1) * HD] = jnp.dot(
                x_ref[...], w_ref[:, cols], preferred_element_type=jnp.float32
            ).astype(jnp.bfloat16)

    pl.semaphore_wait(barrier, members * groups - 1)

    def kv_copy(k, j):
        to_group, to = flip(my_group, j, groups), flip(me, k, members)
        return pltpu.make_async_remote_copy(
            src_ref=sent_ref.at[to, to_group], dst_ref=kv_ref.at[k, j],
            send_sem=kv_send.at[k, j], recv_sem=kv_recv.at[k, j],
            device_id={"cache": to_group, "dev": to}, device_id_type=MESH,
        )

    def near_copy(a, which):
        to = flip(me, a, members)
        return pltpu.make_async_remote_copy(
            src_ref=part_ref.at[flip(to, half * which, members)], dst_ref=near_ref.at[a - 1, which],
            send_sem=near_send.at[a - 1, which], recv_sem=near_recv.at[a - 1, which],
            device_id={"cache": my_group, "dev": to}, device_id_type=MESH,
        )

    def sq_copy(k):
        return pltpu.make_async_remote_copy(
            src_ref=sq_ref, dst_ref=sums_ref.at[k - 1],
            send_sem=sq_send.at[k - 1], recv_sem=sq_recv.at[k - 1],
            device_id={"cache": my_group, "dev": flip(me, k, members)}, device_id_type=MESH,
        )

    for k in (4, 0, 1, 6):
        for j in range(groups):
            if k or j:
                kv_copy(k, j).start()
    for a in range(1, half):
        near_copy(a, 1).start()
    for k in (2, 5, 3, 7):
        for j in range(groups):
            kv_copy(k, j).start()
    for a in range(1, half):
        near_copy(a, 0).start()
    for k in range(1, members):
        sq_copy(k).start()

    split_queries(q_ref, q2_ref, heads, prompt)
    self_pass(q2_ref, self_ref, k2_ref, v2_ref, acc_ref, top_ref, heads, prompt)
    first_key = self_ref[0:1, :HD]
    far = pltpu.make_async_remote_copy(
        src_ref=mid_ref, dst_ref=far_ref, send_sem=far_send, recv_sem=far_recv,
        device_id={"cache": my_group, "dev": flip(me, half, members)}, device_id_type=MESH,
    )
    size = kv_ref.shape[2]
    for pair in range(members // 2):
        for k in (2 * pair, 2 * pair + 1):
            source = flip(me, k, members)
            for j in range(groups):
                if k or j:
                    kv_copy(k, j).wait_recv()
                else:
                    own.wait()
                place = flip(my_group, j, groups)
                neutral(
                    kv_ref[k, j], keep_ref[source, place], first_key, k2_ref, v2_ref,
                    ((k % 2) * groups + j) * size,
                )
        block_pass(q2_ref, k2_ref, v2_ref, acc_ref, top_ref, heads * prompt, 2 * groups * size)
        if pair == 1:
            total = part_ref[flip(me, half, members)].astype(jnp.float32)
            for a in range(1, half):
                near_copy(a, 1).wait_recv()
                total = total + near_ref[a - 1, 1].astype(jnp.float32)
            mid_ref[...] = total.astype(jnp.bfloat16)
            far.start()

    square = sq_ref[...]
    for k in range(1, members):
        sq_copy(k).wait_recv()
        square = square + sums_ref[k - 1]
    inv_rms = jnp.transpose(lax.rsqrt(square / D + eps_norm))[:, :1]
    total = part_ref[me].astype(jnp.float32)
    for a in range(1, half):
        near_copy(a, 0).wait_recv()
        total = total + near_ref[a - 1, 0].astype(jnp.float32)
    far.wait_recv()
    redone = ((total + far_ref[...].astype(jnp.float32)) * inv_rms).astype(jnp.bfloat16)
    neutral(redone, jnp.ones((rec_rows, HD), jnp.bfloat16), first_key, k2_ref, v2_ref, 0)
    block_pass(q2_ref, k2_ref, v2_ref, acc_ref, top_ref, heads * prompt, rec_rows)
    finish(acc_ref, out_ref, heads, prompt)

    for k in range(members):
        for j in range(groups):
            if k or j:
                kv_copy(k, j).wait_send()
    for a in range(1, half):
        near_copy(a, 0).wait_send()
        near_copy(a, 1).wait_send()
    for k in range(1, members):
        sq_copy(k).wait_send()
    far.wait_send()


def remote_attention(q, own_self, keep, x, squares, w, sent):
    prompt, width = q.shape
    heads = width // HD
    members, groups = keep.shape[:2]
    size = sent.shape[2]
    rec_rows = x.shape[0]
    half = members // 2
    vmem = pl.BlockSpec(memory_space=pltpu.VMEM)
    dma = pltpu.SemaphoreType.DMA
    block = (rec_rows, 2 * HD)
    return pl.pallas_call(
        functools.partial(remote_kernel, heads, prompt, groups, members),
        out_shape=jax.ShapeDtypeStruct((prompt, width), jnp.bfloat16),
        in_specs=[vmem] * 6 + [pl.BlockSpec(memory_space=pl.ANY)],
        out_specs=vmem,
        scratch_shapes=state_scratch(heads * prompt, 2 * groups * size) + [
            pltpu.VMEM((members, groups, size, 2 * HD), jnp.bfloat16),
            pltpu.VMEM((members,) + block, jnp.bfloat16),
            pltpu.VMEM((half - 1, 2) + block, jnp.bfloat16),
            pltpu.VMEM(block, jnp.bfloat16),
            pltpu.VMEM(block, jnp.bfloat16),
            pltpu.VMEM((members - 1,) + squares.shape, jnp.float32),
            dma((members, groups)), dma((members, groups)),
            dma((half - 1, 2)), dma((half - 1, 2)), dma, dma,
            dma((members - 1,)), dma((members - 1,)), dma,
        ],
        compiler_params=pltpu.CompilerParams(
            vmem_limit_bytes=61 * 1024 * 1024, collective_id=0, has_side_effects=True
        ),
    )(q, own_self, keep, x, squares, w, sent)


def shards(queries, store_kv, self_kv, rec_states, norm_gain, w_kv, retrieval, doc_home, rec_index):
    groups = lax.axis_size("cache")
    members = lax.axis_size("dev")
    my_group = lax.axis_index("cache")
    my_member = lax.axis_index("dev")
    per_device = QH // members
    my_head = my_member * per_device // (QH // KVH)
    tok, kv_width = store_kv.shape[1:]
    spots = groups * CAP

    docs = jnp.arange(doc_home.shape[0], dtype=jnp.int32)
    stored_at = jnp.sum(
        jnp.where(retrieval[:, :, None] == docs, doc_home[None, None, :], 0), axis=2
    )
    source = stored_at // DOC_GRP
    before = jnp.arange(RET)[None, :] < jnp.arange(RET)[:, None]
    same_home = source[:, :, None] == source[:, None, :]
    rank = jnp.sum((same_home & before[None]).astype(jnp.int32), axis=2)
    places = jnp.arange(CAP, dtype=jnp.int32)
    mine = (source[:, None, :] == my_group) & (rank[:, None, :] == places[None, :, None])
    pick_row = jnp.sum(jnp.where(mine, (stored_at % DOC_GRP)[:, None, :], 0), axis=2)
    sent = gather_blocks(pick_row.reshape(-1), store_kv, groups)

    spot = lax.dynamic_index_in_dim(source * CAP + rank, my_group, 0, keepdims=False)
    held = spot[None, :] == jnp.arange(spots, dtype=jnp.int32)[:, None]
    full = tok * members
    fresh = jnp.all(rec_index[0][:, :, None] != jnp.arange(full, dtype=jnp.int32), axis=1)
    keep = jnp.any(held[:, :, None] & fresh[None], axis=1)
    keep = jnp.transpose(keep.reshape(groups, CAP, members, tok), (2, 0, 1, 3))
    keep = jnp.broadcast_to(
        keep.reshape(members, groups, CAP * tok, 1).astype(jnp.bfloat16),
        (members, groups, CAP * tok, HD),
    )

    own_self = jnp.concatenate(
        [
            lax.dynamic_slice_in_dim(self_kv[0], my_head * HD, HD, 1),
            lax.dynamic_slice_in_dim(self_kv[0], (KVH + my_head) * HD, HD, 1),
        ],
        axis=1,
    )
    states = rec_states[0].astype(jnp.float32)
    squares = jnp.sum(states * states, axis=1)
    if REMOTE and members == KVH and groups * CAP == RET:
        x = (states * norm_gain.astype(jnp.float32)[None, :]).astype(jnp.bfloat16)
        wide = jnp.broadcast_to(squares[None, :], (8, squares.shape[0]))
        return remote_attention(queries[0], own_self, keep, x, wide, w_kv, sent)[None]

    inv_rms = lax.rsqrt(lax.psum(squares, "dev") / D + eps_norm)
    x = (states * norm_gain.astype(jnp.float32)[None, :] * inv_rms[:, None]).astype(jnp.bfloat16)
    summed = lax.psum(jnp.dot(x, w_kv, preferred_element_type=jnp.float32), "dev")
    redone = jnp.concatenate(
        [
            lax.dynamic_slice_in_dim(summed, my_head * HD, HD, 1),
            lax.dynamic_slice_in_dim(summed, (KVH + my_head) * HD, HD, 1),
        ],
        axis=1,
    ).astype(jnp.bfloat16)
    arrived = lax.all_to_all(sent, "cache", split_axis=1, concat_axis=1, tiled=True)
    arrived = jnp.repeat(arrived, members // KVH, axis=0)
    arrived = lax.all_to_all(arrived, "dev", split_axis=0, concat_axis=0, tiled=True)
    out = plain_attention(
        queries[0], own_self, arrived.reshape(-1, 2 * HD), keep.reshape(-1, HD), redone
    )
    return out[None]


def solution(mesh):
    placed = (
        P("cache", None, "dev"),
        P("cache", "dev", None),
        P("cache", None, None),
        P("cache", None, "dev"),
        P("dev"),
        P("dev", None),
        P(),
        P(),
        P("cache", None, None),
    )
    return jax.shard_map(
        shards, mesh=mesh, in_specs=placed, out_specs=P("cache", None, "dev"), check_vma=False
    )
```

time: 947 us -> 214 us (0.23)
  matrix products: 339 us -> 0 us
  blocking collectives: 260 us -> 0 us
  Pallas kernels: 0 us -> 200 us
  other arithmetic: 162 us -> 5.36 us
  local copies, waits for them, and re-layouts: 78.1 us -> 7.77 us
  waiting for transfers between devices: 47.3 us -> 0 us
  loops' own time: 40.3 us -> 0 us
  starting transfers between devices: 11.2 us -> 0 us
    dot_general x66 -> x0, matrix products: 339 us -> none  [the longest x16 159 us: attend(): jnp.einsum('qd,kd->qk', query_block, doc_keys, preferred_element_type=jnp...]
    psum x2 -> x0, blocking collectives: 260 us -> none  [the longest x1 163 us: shards(): lax.psum(jnp.dot(normed, w_kv, preferred_element_type=jnp.float32), 'dev')]
    pallas_call x0 -> x2, Pallas kernels: none -> 200 us  [the longest x1 189 us: remote_attention(): pl.pallas_call(functools.partial(remote_kernel, heads, prompt, groups, me...]
    reduce_sum x35 -> x4, other arithmetic: 146 us -> 2.67 us  [the longest x1 1.3 us: shards(): squares = jnp.sum(states * states, axis=1)]
    all_to_all x2 -> x0, waiting for transfers between devices: 47.3 us -> none  [the longest x1 47.3 us: shards(): lax.all_to_all(outgoing, 'cache', split_axis=0, concat_axis=0, tiled=True)]
    another operation x1 -> x0, loops' own time: 40.3 us -> none  [shards(): lax.map(attend, jnp.arange(per_device * block_count, dtype=jnp.int32))]
    while x64 -> x0, local copies, waits for them, and re-layouts: 21.1 us -> none
    gather x5 -> x0, local copies, waits for them, and re-layouts: 17.2 us -> none  [the longest x1 6.12 us: shards(): jnp.take(store_kv, pick_row.reshape(-1), axis=0)]
  transfers between devices with their start and end apart: 2 -> 0, of which waited for: 1 -> 0; matrix products, arithmetic and copies ran while one was open for 2% -> 0% of each run, Pallas kernels for 0% -> 0%
where the time goes in v1:
time: 214 us; the launch traced here: 213 us
  Pallas kernels  200 us (93%)
  local copies, waits for them, and re-layouts  7.77 us (4%)
  other arithmetic  5.36 us (3%)
    pallas_call x1, Pallas kernels, remote_attention(): pl.pallas_call(functools.partial(remote_kernel, heads, prompt, groups, me...  189 us
    pallas_call x1, Pallas kernels, gather_blocks(): pl.pallas_call(gather_kernel, grid_spec=pltpu.PrefetchScalarGridSpec(num_...  11 us

profile of v1, /device:TPU:17, one launch (start us, length us, event | category | flops | bytes accessed | tf_op | source)
XLA Modules:
  0.0 213.1 jit_solution(14235535405262419113)
XLA Ops:
  0.0 0.0 copy-start
  0.0 1.0 select_reduce_fusion
  1.0 0.2 convert_reduce_fusion
  1.3 0.2 select_reduce_fusion.1
  1.4 0.6 reshape.110.rows_ref
  2.1 0.7 convert_element_type.39
  2.7 0.9 fusion.2
  3.7 0.2 and_reduce_fusion
  3.9 0.1 reshape.113
  4.0 0.1 reshape.114
  4.1 1.1 dynamic-slice_bitcast_fusion.1
  5.2 0.8 pad_maximum_fusion.self_ref
  6.0 0.0 copy-done
  6.0 1.3 fusion.1
  7.3 0.6 broadcast_in_dim.33.sq_ref
  7.9 2.2 %broadcast_in_dim.32.keep_ref = bf16[8,4,256,128]{3,2,1,0:T(8,128)(2,1)} broadcast(bf16[8,4,256]{2,1,0:T(4,128)(2,1)S(1)} %reshape.114), dimensions={0,1,2} | broadcast | bytes 2113536 | tf_op jit(solution)/shard_map/broadcast_in_dim | solution.py:366
  10.1 11.0 %shard_map.91.sent_ref = bf16[8,4,256,256]{3,2,1,0:T(8,128)(2,1)} custom-call(s32[16]{0:T(128)} %reshape.110.rows_ref, bf16[32,64,2048]{2,1,0:T(8,128)(2,1)} %store_ref.1), custom_call_target="tpu_custom_call" | custom-call | tf_op jit(solution)/shard_map/pallas_call | solution.py:46
  21.2 188.8 %shard_map.92 = bf16[1024,1024]{1,0:T(8,128)(2,1)} custom-call(bf16[1024,1024]{1,0:T(8,128)(2,1)} %bitcast.15, bf16[1024,256]{1,0:T(8,128)(2,1)} %pad_maximum_fusion.self_ref, bf16[8,4,256,128]{3,2,1,0:T(8,128)(2,1)} %broadcast_in_dim.32.keep_ref, bf16[512,1024]{1,0:T(8,128)(2,1)} %get-tuple-element.10.x_ref, f32[8,512]{1,0:T(8,128)} %broadcast_in_dim.33.sq_ref, ...), custom_call_target="tpu_custom_call" | custom-call | tf_op jit(solution)/shard_map/pallas_call | solution.py:315
  210.0 3.1 %copy.17 = bf16[1,1024,1024]{2,1,0:T(8,128)(2,1)} copy(bf16[1,1024,1024]{2,1,0:T(8,128)(2,1)} %bitcast.14) | data formatting | bytes 4194304
  (8 shorter events, 0.1 us)
Async XLA Ops:
  0.0 6.0 %copy-start = (bf16[1,512,1024]{2,1,0:T(8,128)(2,1)S(1)}, bf16[1,512,1024]{2,1,0:T(8,128)(2,1)}, u32[]{:S(2)}) copy-start(bf16[1,512,1024]{2,1,0:T(8,128)(2,1)} %param.12) | copy-start | bytes 3145732

commit v2 on v1

--- a/solution.py
+++ b/solution.py
@@ -35,26 +35,32 @@
     return out
 
 
-def gather_kernel(rows_ref, store_ref, out_ref):
-    for head in range(KVH):
-        out_ref[head, 0, :, :HD] = store_ref[0, :, head * HD : (head + 1) * HD]
-        out_ref[head, 0, :, HD:] = store_ref[0, :, (KVH + head) * HD : (KVH + head + 1) * HD]
+def gather_kernel(rows_ref, *refs):
+    out_ref = refs[-1]
+    tok = refs[0].shape[1]
+    for place, store_ref in enumerate(refs[:-1]):
+        span = slice(place * tok, (place + 1) * tok)
+        for head in range(KVH):
+            out_ref[head, 0, span, :HD] = store_ref[0, :, head * HD : (head + 1) * HD]
+            out_ref[head, 0, span, HD:] = store_ref[0, :, (KVH + head) * HD : (KVH + head + 1) * HD]
 
 
 def gather_blocks(pick_row, store_kv, groups):
     tok, width = store_kv.shape[1:]
+
+    def spec(place):
+        return pl.BlockSpec((1, tok, width), lambda i, rows: (rows[i * CAP + place], 0, 0))
+
     return pl.pallas_call(
         gather_kernel,
         grid_spec=pltpu.PrefetchScalarGridSpec(
             num_scalar_prefetch=1,
-            grid=(groups * CAP,),
-            in_specs=[pl.BlockSpec((1, tok, width), lambda i, rows: (rows[i], 0, 0))],
-            out_specs=pl.BlockSpec(
-                (KVH, 1, tok, 2 * HD), lambda i, rows: (0, i // CAP, i % CAP, 0)
-            ),
+            grid=(groups,),
+            in_specs=[spec(place) for place in range(CAP)],
+            out_specs=pl.BlockSpec((KVH, 1, CAP * tok, 2 * HD), lambda i, rows: (0, i, 0, 0)),
         ),
         out_shape=jax.ShapeDtypeStruct((KVH, groups, CAP * tok, 2 * HD), store_kv.dtype),
-    )(pick_row, store_kv)
+    )(pick_row, *[store_kv] * CAP)
 
 
 def nt(a, b):
@@ -95,7 +101,7 @@
             top_ref[rows, :] = jnp.broadcast_to(top, (TQ, HD))
 
 
-def block_pass(q2_ref, k2_ref, v2_ref, acc_ref, top_ref, rows_total, count, unroll=2):
+def block_pass(q2_ref, k2_ref, v2_ref, acc_ref, top_ref, rows_total, count, unroll=4):
     @pl.loop(0, rows_total // (TQ * unroll))
     def _(step):
         spans = [

time: 214 us -> 187 us (0.87)
  Pallas kernels: 200 us -> 174 us
    pallas_call x1, Pallas kernels: 189 us -> 168 us  [remote_attention(): pl.pallas_call(functools.partial(remote_kernel, heads, prompt, groups, me...]
    pallas_call x1, Pallas kernels: 11 us -> 5.59 us  [gather_blocks(): pl.pallas_call(gather_kernel, grid_spec=pltpu.PrefetchScalarGridSpec(num_...]
where the time goes in v2:
time: 187 us
  Pallas kernels  174 us (93%)
  local copies, waits for them, and re-layouts  7.77 us (4%)
  other arithmetic  5.36 us (3%)
    pallas_call x1, Pallas kernels, remote_attention(): pl.pallas_call(functools.partial(remote_kernel, heads, prompt, groups, me...  168 us
    pallas_call x1, Pallas kernels, gather_blocks(): pl.pallas_call(gather_kernel, grid_spec=pltpu.PrefetchScalarGridSpec(num_...  5.59 us

profile of v2, /device:TPU:17, one launch (start us, length us, event | category | flops | bytes accessed | tf_op | source)
XLA Modules:
  0.0 187.0 jit_solution(3341808361083581164)
XLA Ops:
  0.0 0.0 copy-start
  0.0 1.0 select_reduce_fusion
  1.0 0.2 convert_reduce_fusion
  1.3 0.2 select_reduce_fusion.1
  1.4 0.6 reshape.110.rows_ref
  2.1 0.7 convert_element_type.39
  2.7 0.9 fusion.2
  3.7 0.2 and_reduce_fusion
  3.9 0.1 reshape.113
  4.0 0.1 reshape.114
  4.1 1.1 dynamic-slice_bitcast_fusion.1
  5.2 0.8 pad_maximum_fusion.self_ref
  6.0 0.0 copy-done
  6.0 1.3 fusion.1
  7.3 0.6 broadcast_in_dim.33.sq_ref
  7.9 2.2 %broadcast_in_dim.32.keep_ref = bf16[8,4,256,128]{3,2,1,0:T(8,128)(2,1)} broadcast(bf16[8,4,256]{2,1,0:T(4,128)(2,1)S(1)} %reshape.114), dimensions={0,1,2} | broadcast | bytes 2113536 | tf_op jit(solution)/shard_map/broadcast_in_dim | solution.py:372
  10.1 5.6 %shard_map.91.sent_ref = bf16[8,4,256,256]{3,2,1,0:T(8,128)(2,1)} custom-call(s32[16]{0:T(128)} %reshape.110.rows_ref, bf16[32,64,2048]{2,1,0:T(8,128)(2,1)} %refs_3_.1, bf16[32,64,2048]{2,1,0:T(8,128)(2,1)} %refs_3_.1, bf16[32,64,2048]{2,1,0:T(8,128)(2,1)} %refs_3_.1, bf16[32,64,2048]{2,1,0:T(8,128)(2,1)} %refs_3_.1), custom_call_target="tpu_custom_call" | custom-call | tf_op jit(solution)/shard_map/pallas_call | solution.py:54
  15.7 168.2 %shard_map.92 = bf16[1024,1024]{1,0:T(8,128)(2,1)} custom-call(bf16[1024,1024]{1,0:T(8,128)(2,1)} %bitcast.15, bf16[1024,256]{1,0:T(8,128)(2,1)} %pad_maximum_fusion.self_ref, bf16[8,4,256,128]{3,2,1,0:T(8,128)(2,1)} %broadcast_in_dim.32.keep_ref, bf16[512,1024]{1,0:T(8,128)(2,1)} %get-tuple-element.10.x_ref, f32[8,512]{1,0:T(8,128)} %broadcast_in_dim.33.sq_ref, ...), custom_call_target="tpu_custom_call" | custom-call | tf_op jit(solution)/shard_map/pallas_call | solution.py:321
  183.9 3.1 %copy.17 = bf16[1,1024,1024]{2,1,0:T(8,128)(2,1)} copy(bf16[1,1024,1024]{2,1,0:T(8,128)(2,1)} %bitcast.14) | data formatting | bytes 4194304
  (8 shorter events, 0.1 us)
Async XLA Ops:
  0.0 6.0 %copy-start = (bf16[1,512,1024]{2,1,0:T(8,128)(2,1)S(1)}, bf16[1,512,1024]{2,1,0:T(8,128)(2,1)}, u32[]{:S(2)}) copy-start(bf16[1,512,1024]{2,1,0:T(8,128)(2,1)} %param.12) | copy-start | bytes 3145732
